TPU v7x, 32 devices: a whole 2x2x4 slice. The times are simulated.
32 devices in a mesh: img: 2 (over core), fsdp: 16 (over z, y, x).
Axes of the slice: x: 2, y: 2, z: 4, core: 2. Of those that a mesh axis runs over, the one named last changes fastest.
Arguments:
- text_states: bfloat16 [4096, 8192], P('fsdp')
- text_gain: float32 [8192], replicated, may hold values from 0.1 to 1.9
- vision: bfloat16 [2, 128, 8192], P('img', 'fsdp'), may hold values from -6 to 6
- q_weight: bfloat16 [8192, 1024], P('fsdp', 'img'), may hold values from -0.0625 to 0.0625
- k_weight: bfloat16 [8192, 256], P('fsdp', 'img'), may hold values from -0.0625 to 0.0625
- v_weight: bfloat16 [8192, 256], P('fsdp', 'img'), may hold values from -0.0625 to 0.0625
- q_gain: float32 [128], replicated, may hold values from 1 to 16
- k_gain: float32 [128], replicated, may hold values from 1 to 16
- owners: int32 [64, 4], P('fsdp'), may hold values from 0 to 1
- counts: int32 [64], P('fsdp'), may hold values from 0 to 4
- gate_value: float32 [1], replicated, may hold values from 0.3 to 1.5
Outputs:
- attended: bfloat16 [4096, 1024], P('fsdp', 'img')
All inputs are finite; a program needn't handle non-finite values.
Results may differ from a plain program's by a relative error of at most 0.025.
The roundings to bfloat16 on the way count: a program that leaves them out, or rounds other values in their place, can miss the bound.
Values may be sent and summed in bfloat16 or wider, within the bound.
A program may use at most 64 MiB of HBM per device.

v0:
```python
import jax
import jax.numpy as jnp
from jax import lax
from jax.sharding import PartitionSpec as P

norm_epsilon = 1e-05
masked_score = -1e30


def head_norm(values, gain):
    mean_square = jnp.mean(values * values, axis=-1, keepdims=True)
    return values * lax.rsqrt(mean_square + norm_epsilon) * gain


def on_device(
    text_states,
    text_gain,
    vision,
    q_weight,
    k_weight,
    v_weight,
    q_gain,
    k_gain,
    owners,
    counts,
    gate_value,
):
    token_rows = text_states.shape[0]
    width = text_states.shape[1]
    head_size = q_gain.shape[0]
    per_group = q_weight.shape[1] // head_size
    images = lax.axis_size("img")
    shard_tokens = vision.shape[1]
    text_float = text_states.astype(jnp.float32)
    normed = (
        text_float
        * lax.rsqrt(jnp.mean(text_float * text_float, axis=-1, keepdims=True) + norm_epsilon)
        * text_gain
    ).astype(jnp.bfloat16)
    visual = lax.all_gather(vision, "img", axis=0, tiled=True).reshape(images * shard_tokens, width)
    columns = visual
    joined = jnp.concatenate(
        (
            lax.all_gather(k_weight, "fsdp", axis=0, tiled=True),
            lax.all_gather(v_weight, "fsdp", axis=0, tiled=True),
        ),
        axis=1,
    )
    pair_full = jnp.dot(columns, joined, preferred_element_type=jnp.float32)
    columns = normed
    query_full = jnp.dot(
        columns,
        lax.all_gather(q_weight, "fsdp", axis=0, tiled=True),
        preferred_element_type=jnp.float32,
    )
    row_count = token_rows * per_group
    queries = (
        head_norm(query_full.reshape(token_rows, per_group, head_size), q_gain)
        .astype(jnp.bfloat16)
        .reshape(row_count, head_size)
    )
    keys = (
        head_norm(pair_full[:, :head_size], k_gain)
        .astype(jnp.bfloat16)
        .reshape(images, shard_tokens, head_size)
    )
    values = pair_full[:, head_size:].astype(jnp.bfloat16).reshape(images, shard_tokens, head_size)
    block_count = owners.shape[0]
    live_slot = jnp.arange(owners.shape[1], dtype=jnp.int32)[None, :] < counts[:, None]
    matched = (
        owners[:, :, None] == jnp.arange(images, dtype=jnp.int32)[None, None, :]
    ) & live_slot[:, :, None]
    block_images = jnp.any(matched, axis=1)
    token_images = jnp.broadcast_to(
        block_images[:, None, :], (block_count, token_rows // block_count, images)
    ).reshape(token_rows, images)
    row_live = jnp.any(token_images, axis=1)
    score_scale = head_size ** (-0.5)
    key_piece = lax.all_gather(keys, "fsdp", axis=1, tiled=True)
    value_piece = lax.all_gather(values, "fsdp", axis=1, tiled=True)
    key_count = key_piece.shape[1]
    allowed = jnp.broadcast_to(token_images[:, :, None], (token_rows, images, key_count)).reshape(
        token_rows, images * key_count
    )
    running_max = jnp.full((row_count,), masked_score, jnp.float32)
    scores = (
        jnp.einsum(
            "rd,kd->rk",
            queries,
            key_piece.reshape(images * key_count, head_size),
            preferred_element_type=jnp.float32,
        )
        * score_scale
    )
    scores = jnp.where(
        allowed[:, None, :], scores.reshape(token_rows, per_group, -1), masked_score
    ).reshape(row_count, -1)
    new_max = jnp.maximum(running_max, jnp.max(scores, axis=1))
    weights = jnp.exp(scores - new_max[:, None]).astype(jnp.bfloat16)
    denominator = jnp.sum(weights.astype(jnp.float32), axis=1)
    numerator = jnp.dot(
        weights,
        value_piece.reshape(images * key_count, head_size),
        preferred_element_type=jnp.float32,
    )
    running_max, denominator, numerator = (new_max, denominator, numerator)
    live_rows = jnp.broadcast_to(row_live[:, None], (token_rows, per_group)).reshape(row_count)
    safe_denominator = jnp.where(live_rows, denominator, jnp.float32(1.0))
    factor = jnp.where(live_rows, jnp.tanh(gate_value[0]), jnp.float32(0.0))
    attended = numerator / safe_denominator[:, None] * factor[:, None]
    return attended.reshape(token_rows, per_group * head_size).astype(jnp.bfloat16)


def solution(mesh):
    in_specs = (
        P("fsdp", None),
        P(),
        P("img", "fsdp", None),
        P("fsdp", "img"),
        P("fsdp", "img"),
        P("fsdp", "img"),
        P(),
        P(),
        P("fsdp", None),
        P("fsdp"),
        P(),
    )
    out_specs = P("fsdp", "img")
    return jax.shard_map(
        on_device, mesh=mesh, in_specs=in_specs, out_specs=out_specs, check_vma=False
    )
```

profile of v0, /device:TPU:0, one launch (start us, length us, event | category | flops | bytes accessed | tf_op | source)
XLA Modules:
  0.0 267.7 jit_solution(7591091311817405118)
XLA Ops:
  6.5 0.0 copy-start
  6.5 0.0 all-gather.6.cloned.1.call-start
  6.5 0.7 all-gather.6.cloned.1.call-update
  7.3 0.0 all-gather.8.cloned.1.call-start
  7.3 0.7 all-gather.8.cloned.1.call-update
  8.0 0.0 all-gather.4.cloned.1.call-start
  8.1 0.7 all-gather.4.cloned.1.call-update
  8.7 0.7 iota_compare_fusion.1
  9.5 0.9 fusion.24
  10.4 0.1 broadcast_in_dim.66
  10.5 0.1 broadcast_in_dim.67
  10.6 0.2 copy.22
  10.8 0.2 broadcast_in_dim.70
  11.0 0.2 broadcast_in_dim.71
  11.3 0.3 copy.25
  11.6 0.1 reduce_or.22
  11.7 0.1 broadcast_in_dim.74
  11.8 0.1 broadcast_in_dim.75
  11.9 0.1 reshape.111
  12.7 2.3 all_gather.21
  15.0 3.1 %fusion = f32[256]{0:T(256)S(1)} fusion(bf16[256,8192]{1,0:T(8,128)(2,1)} %param.11), kind=kLoop, calls=%fused_computation.2 | loop fusion | flops 6291200 | bytes 4195328 | tf_op jit(solution)/shard_map/reduce_sum | solution.py:37
  18.1 0.0 copy-start.1
  18.1 0.0 copy-start.2
  18.1 0.0 copy-done
  18.2 55.4 %all-gather.6.cloned.1.call-done = bf16[8192,128]{1,0:T(8,128)(2,1)} async-done(((bf16[512,128]{1,0:T(8,128)(2,1)}), bf16[8192,128]{1,0:T(8,128)(2,1)}) %all-gather.6.cloned.1.call-update) | async-done | bytes 2097168 | tf_op jit(solution)/shard_map/all_gather | solution.py:44
  73.6 62.2 %all-gather.8.cloned.1.call-done = bf16[8192,128]{1,0:T(8,128)(2,1)} async-done(((bf16[512,128]{1,0:T(8,128)(2,1)}), bf16[8192,128]{1,0:T(8,128)(2,1)}) %all-gather.8.cloned.1.call-update) | async-done | bytes 2097168 | tf_op jit(solution)/shard_map/all_gather | solution.py:45
  135.7 2.9 %fusion.14 = f32[16,256]{1,0:T(8,128)S(1)} fusion(bf16[8192,128]{1,0:T(8,128)(2,1)} %all-gather.8.cloned.1.call-done, bf16[8192,128]{1,0:T(8,128)(2,1)} %all-gather.6.cloned.1.call-done, bf16[2,8,8192]{2,1,0:T(8,128)(2,1)S(1)} %all_gather.21), kind=kOutput, calls=%fused_computation.17 | convolution fusion | flops 75497472 | bytes 4472832 | tf_op jit(solution)/shard_map/dot_general | solution.py:49
  138.6 0.1 multiply_reduce_fusion
  138.7 0.0 copy-done.1
  138.7 0.1 fusion.20
  138.8 39.4 %all_gather.22 = bf16[2,128,128]{2,1,0:T(8,128)(2,1)S(1)} all-gather(bf16[2,8,128]{2,1,0:T(8,128)(2,1)S(1)} %fusion.20), channel_id=1, replica_groups=mesh['img'=2,'fsdp'=16] {'fsdp'}, dimensions={1}, use_global_device_ids=true | all-gather | bytes 69632 | tf_op jit(solution)/shard_map/all_gather | solution.py:79
  178.2 36.5 %all_gather.23 = bf16[2,128,128]{2,1,0:T(8,128)(2,1)S(1)} all-gather(bf16[2,8,128]{2,1,0:T(8,128)(2,1)S(1)} %fusion.21), channel_id=1, replica_groups=mesh['img'=2,'fsdp'=16] {'fsdp'}, dimensions={1}, use_global_device_ids=true | all-gather | bytes 69632 | tf_op jit(solution)/shard_map/all_gather | solution.py:80
  214.8 36.3 %all-gather.4.cloned.1.call-done = bf16[8192,512]{1,0:T(8,128)(2,1)} async-done(((bf16[512,512]{1,0:T(8,128)(2,1)}), bf16[8192,512]{1,0:T(8,128)(2,1)}) %all-gather.4.cloned.1.call-update) | async-done | bytes 8388624 | tf_op jit(solution)/shard_map/all_gather | solution.py:53
  251.0 0.0 copy-done.2
  251.0 7.0 %fusion.26 = (f32[256,512]{1,0:T(8,128)S(1)}, f32[256,512]{1,0:T(8,128)S(1)}) fusion(bf16[8192,512]{1,0:T(8,128)(2,1)} %all-gather.4.cloned.1.call-done, bf16[256,8192]{1,0:T(8,128)(2,1)} %param.11, f32[8192]{0:T(1024)S(1)} %copy-done.2, f32[256]{0:T(256)S(1)} %add_rsqrt_fusion.1), kind=kOutput, calls=%fused_computation.42 | convolution fusion | flops 2156003328 | bytes 13665280 | tf_op jit(solution)/shard_map/dot_general | solution.py:51
  258.1 0.2 mul.90
  258.3 0.3 reduce_sum.37
  258.7 0.3 mul.91
  259.0 0.1 fusion.18
  259.1 0.2 convert_element_type.32
  259.3 0.3 fusion.27
  259.6 0.2 convert_reduce_fusion
  259.8 0.5 fusion.13
  260.3 0.9 convert_element_type.37
  (8 shorter events, 0.1 us)
Async XLA Ops:
  6.5 11.6 %copy-start = (f32[128]{0:T(128)S(1)}, f32[128]{0:T(128)}, u32[]{:S(2)}) copy-start(f32[128]{0:T(128)} %param.17) | copy-start | bytes 1540
  6.5 67.0 %all-gather.6.cloned.1.call-start = ((), (), s32[]{:S(2)}) async-start(), calls=%async_computation.1 | async-start | bytes 2228224 | tf_op jit(solution)/shard_map/all_gather | solution.py:44
  7.3 128.5 %all-gather.8.cloned.1.call-start = ((), (), s32[]{:S(2)}) async-start(), calls=%async_computation.2 | async-start | bytes 2228224 | tf_op jit(solution)/shard_map/all_gather | solution.py:45
  8.0 243.0 %all-gather.4.cloned.1.call-start = ((), (), s32[]{:S(2)}) async-start(), calls=%async_computation | async-start | bytes 8912896 | tf_op jit(solution)/shard_map/all_gather | solution.py:53
  18.1 120.6 %copy-start.1 = (f32[128]{0:T(128)S(1)}, f32[128]{0:T(128)}, u32[]{:S(2)}) copy-start(f32[128]{0:T(128)} %param.18) | copy-start | bytes 1540
  18.1 232.9 %copy-start.2 = (f32[8192]{0:T(1024)S(1)}, f32[8192]{0:T(1024)}, u32[]{:S(2)}) copy-start(f32[8192]{0:T(1024)} %param.12) | copy-start | bytes 98308
Sparse Core Ops, SparseCore 0:
  10.1 63.3 all-gather.5
  76.3 59.3 all-gather.7
  138.5 112.5 all-gather.3
where the time goes:
time: 268 us
  waiting for transfers between devices  156 us (58%)
  blocking collectives  78.3 us (29%)
  between operations  14 us (5%)
  matrix products  10.8 us (4%)
  other arithmetic  5.62 us (2%)
  local copies, waits for them, and re-layouts  3.13 us (1%)
    all_gather x1, waiting for transfers between devices, on_device(): lax.all_gather(v_weight, 'fsdp', axis=0, tiled=True)  62.2 us
    all_gather x1, waiting for transfers between devices, on_device(): lax.all_gather(k_weight, 'fsdp', axis=0, tiled=True)  55.4 us
    all_gather x1, blocking collectives, on_device(): key_piece = lax.all_gather(keys, 'fsdp', axis=1, tiled=True)  39.4 us
    all_gather x1, blocking collectives, on_device(): value_piece = lax.all_gather(values, 'fsdp', axis=1, tiled=True)  36.5 us
    all_gather x1, waiting for transfers between devices, on_device(): lax.all_gather(q_weight, 'fsdp', axis=0, tiled=True)  36.3 us
    dot_general x1, matrix products, on_device(): jnp.dot(columns, lax.all_gather(q_weight, 'fsdp', axis=0, tiled=True), pr...  7.04 us
  transfers between devices with their start and end apart: 3, of which 3 were waited for; matrix products, arithmetic and copies ran while one was open for 4% of the time, Pallas kernels for 0%

commit v1 on v0

v1 whole, which is shorter than its diff:
```python
import functools

import jax
import jax.numpy as jnp
from jax import lax
from jax.experimental import pallas as pl
from jax.experimental.pallas import tpu as pltpu
from jax.sharding import PartitionSpec as P

norm_epsilon = 1e-05
masked_score = -1e30
MESH = pl.DeviceIdType.MESH
row_tile = 16


def head_norm(values, gain):
    mean_square = jnp.mean(values * values, axis=-1, keepdims=True)
    return values * lax.rsqrt(mean_square + norm_epsilon) * gain


def kernel(
    images, shards, group, halves,
    text_ref, gain_ref, vision_ref, q_ref, k_ref, v_ref, qg_ref, kg_ref, owners_ref, counts_ref, gate_ref,
    out_ref,
    normed, others, wbuf, total, part_send, part_recv,
    vis_send, vis_all, pair_send, pair_recv, kv_own, kv_all,
    w_send, w_recv, t_send, t_recv, f_send, f_recv, p_send, p_recv, v_send, v_recv, s_send, s_recv,
):
    img = lax.axis_index("img")
    me = lax.axis_index("fsdp")
    line = shards // group
    along = lax.div(me, group)
    member = lax.rem(me, group)
    rows, width = text_ref.shape
    depth, columns = q_ref.shape
    half = columns // halves
    head = qg_ref.shape[1]
    tokens = vision_ref.shape[1]
    part_rows = rows // images

    def copy(src, dst, send, recv, target):
        return pltpu.make_async_remote_copy(
            src_ref=src, dst_ref=dst, send_sem=send, recv_sem=recv, device_id=target, device_id_type=MESH
        )

    def drain(ref, sem):
        pltpu.make_async_copy(ref, ref, sem).wait()

    barrier = pltpu.get_barrier_semaphore()

    def greet(step, carry):
        pl.semaphore_signal(barrier, inc=1, device_id={"fsdp": lax.rem(me + step, shards)}, device_id_type=MESH)
        return carry

    lax.fori_loop(1, shards, greet, 0)
    for j in range(1, images):
        pl.semaphore_signal(barrier, inc=1, device_id={"img": lax.rem(img + j, images)}, device_id_type=MESH)
    for h in range(halves):
        wbuf[h, along] = q_ref[:, h * half : (h + 1) * half]
    for f in range(shards):
        vis_send[f] = vision_ref[0, :, f * depth : (f + 1) * depth].astype(jnp.float32)
    vis_all[img, me] = vis_send[me]
    pl.semaphore_wait(barrier, shards - 1 + images - 1)

    def w_copy(h, step, way):
        slot = along - step if way == 0 else along + step
        to = me + group if way == 0 else me - group
        return copy(
            wbuf.at[h, slot], wbuf.at[h, slot], w_send.at[h, step, way], w_recv.at[h, step, way], {"fsdp": to}
        )

    def w_sends(step, way):
        if way == 0:
            return (along - step >= 0) & (along + 1 < line)
        return (along + step < line) & (along >= 1)

    def w_gets(step, way):
        if way == 0:
            return along - 1 - step >= 0
        return along + 1 + step < line

    def w_start(h, step):
        for way in range(2):
            @pl.when(w_sends(step, way))
            def _():
                w_copy(h, step, way).start()

    def w_arrive(h, step):
        for way in range(2):
            @pl.when(w_gets(step, way))
            def _():
                w_copy(h, step, way).wait_recv()
        if step + 1 < line - 1:
            w_start(h, step + 1)

    def spread(source, target, send, recv):
        def one(step, carry):
            to = lax.rem(me + step, shards)
            copy(source(to), target, send, recv, {"fsdp": to}).start()
            return carry

        lax.fori_loop(1, shards, one, 0)

    w_start(0, 0)
    spread(lambda to: vis_send.at[to], vis_all.at[img, me], v_send.at[0], v_recv.at[0])

    def scale_of(row):
        acc = jnp.zeros((row_tile, depth), jnp.float32)
        for f in range(shards):
            x = text_ref[pl.ds(row, row_tile), f * depth : (f + 1) * depth].astype(jnp.float32)
            acc = acc + x * x
        return lax.rsqrt(jnp.sum(acc, axis=1, keepdims=True) / width + norm_epsilon)

    def norm_all(t, carry):
        row = pl.multiple_of(img * part_rows + t * row_tile, row_tile)
        scale = scale_of(row)
        for f in range(shards):
            span = slice(f * depth, (f + 1) * depth)
            x = text_ref[pl.ds(row, row_tile), span].astype(jnp.float32)
            place = f // group * depth
            normed[f % group, pl.ds(row, row_tile), place : place + depth] = (x * scale * gain_ref[:, span]).astype(
                jnp.bfloat16
            )
        return carry

    lax.fori_loop(0, part_rows // row_tile, norm_all, 0)
    mine = pl.ds(pl.multiple_of(img * part_rows, part_rows), part_rows)

    def t_copy(d):
        to = lax.rem(member + d, group)
        return copy(
            normed.at[to, mine], others.at[d - 1, mine], t_send.at[d - 1], t_recv.at[d - 1],
            {"fsdp": along * group + to},
        )

    for d in range(1, group):
        t_copy(d).start()

    for j in range(1, images):
        def norm_own(t, carry):
            row = pl.multiple_of(lax.rem(img + j, images) * part_rows + t * row_tile, row_tile)
            scale = scale_of(row)
            for a in range(line):
                span = pl.ds(pl.multiple_of((a * group + member) * depth, depth), depth)
                x = text_ref[pl.ds(row, row_tile), span].astype(jnp.float32)
                normed[member, pl.ds(row, row_tile), a * depth : (a + 1) * depth] = (
                    x * scale * gain_ref[:, span]
                ).astype(jnp.bfloat16)
            return carry

        lax.fori_loop(0, part_rows // row_tile, norm_own, 0)

    drain(vis_all.at[img, pl.ds(0, shards - 1)], v_recv.at[0])

    def s_copy(j):
        return copy(
            vis_all.at[img], vis_all.at[img], s_send.at[j - 1], s_recv.at[j - 1], {"img": lax.rem(img + j, images)}
        )

    for j in range(1, images):
        s_copy(j).start()
    w_arrive(0, 0)
    w_start(1, 0)
    for j in range(1, images):
        s_copy(j).wait_recv()
    for m in range(images):
        x = vis_all[m].reshape(shards * tokens, depth).astype(jnp.bfloat16)
        keys_part = jnp.dot(x, k_ref[...], preferred_element_type=jnp.float32)
        values_part = jnp.dot(x, v_ref[...], preferred_element_type=jnp.float32)
        pair_send[:, m, :, :head] = keys_part.reshape(shards, tokens, head)
        pair_send[:, m, :, head:] = values_part.reshape(shards, tokens, head)
    spread(lambda to: pair_send.at[to], pair_recv.at[me], v_send.at[1], v_recv.at[1])
    pair_recv[me] = pair_send[me]
    for step in range(1, line - 1):
        w_arrive(0, step)
        if step == 1:
            drain(pair_recv.at[pl.ds(0, shards - 1)], v_recv.at[1])
            pair = jnp.sum(pair_recv[...], axis=0).reshape(images * tokens, 2 * head)
            kv_own[:, :head] = head_norm(pair[:, :head], kg_ref[...]).astype(jnp.bfloat16)
            kv_own[:, head:] = pair[:, head:].astype(jnp.bfloat16)
            spread(lambda to: kv_own, kv_all.at[me], v_send.at[2], v_recv.at[2])
            kv_all[me] = kv_own[...]
    w_arrive(1, 0)

    def f_copy(d, j):
        return copy(
            others.at[d - 1, mine], others.at[d - 1, mine], f_send.at[d - 1, j - 1], f_recv.at[d - 1, j - 1],
            {"img": lax.rem(img + j, images)},
        )

    for d in range(1, group):
        t_copy(d).wait_recv()
        for j in range(1, images):
            f_copy(d, j).start()
    for d in range(1, group):
        for j in range(1, images):
            f_copy(d, j).wait_recv()

    def p_copy(h, d):
        to = lax.rem(member + group - d, group)
        return copy(
            part_send.at[h, d - 1], part_recv.at[h, d - 1], p_send.at[h, d - 1], p_recv.at[h, d - 1],
            {"fsdp": along * group + to},
        )

    def project(h):
        weight = wbuf[h].reshape(line * depth, half)
        for d in range(1, group):
            part_send[h, d - 1] = jnp.dot(others[d - 1], weight, preferred_element_type=jnp.float32)
            p_copy(h, d).start()
        total[h] = jnp.dot(normed[member], weight, preferred_element_type=jnp.float32)

    project(0)
    for step in range(1, line - 1):
        w_arrive(1, step)
    project(1)

    drain(kv_all.at[pl.ds(0, shards - 1)], v_recv.at[2])
    key_count = shards * images * tokens
    blocks = owners_ref.shape[0]
    key_image = lax.rem(lax.div(lax.broadcasted_iota(jnp.int32, (1, key_count), 1), tokens), images)
    gate = jnp.tanh(gate_ref[...])
    masks, factors = [], []
    for blk in range(blocks):
        row = jnp.zeros((1, key_count), jnp.int32)
        live = jnp.int32(0)
        for m in range(images):
            hit = jnp.int32(0)
            for slot in range(owners_ref.shape[1]):
                same = jnp.where(owners_ref[blk, slot] == m, 1, 0)
                hit = jnp.maximum(hit, jnp.where(slot < counts_ref[blk], same, 0))
            row = jnp.where(key_image == m, hit, row)
            live = jnp.maximum(live, hit)
        masks.append(jnp.broadcast_to(row, (rows // blocks, key_count)))
        factors.append(jnp.broadcast_to(gate * live.astype(jnp.float32), (rows // blocks, 1)))
    allowed = jnp.concatenate(masks, axis=0) > 0
    factor = jnp.concatenate(factors, axis=0)
    pairs = kv_all[...].reshape(key_count, 2 * head)
    keys, values = pairs[:, :head], pairs[:, head:]
    for h in range(halves):
        for d in range(1, group):
            p_copy(h, d).wait_recv()
        full = total[h]
        for d in range(1, group):
            full = full + part_recv[h, d - 1]
        for n in range(half // head):
            queries = head_norm(full[:, n * head : (n + 1) * head], qg_ref[...]).astype(jnp.bfloat16)
            scores = lax.dot_general(
                queries, keys, (((1,), (1,)), ((), ())), preferred_element_type=jnp.float32
            ) * head ** (-0.5)
            scores = jnp.where(allowed, scores, masked_score)
            weights = jnp.exp(scores - jnp.max(scores, axis=1, keepdims=True)).astype(jnp.bfloat16)
            denominator = jnp.sum(weights.astype(jnp.float32), axis=1, keepdims=True)
            numerator = jnp.dot(weights, values, preferred_element_type=jnp.float32)
            place = h * half + n * head
            out_ref[:, place : place + head] = (numerator / denominator * factor).astype(jnp.bfloat16)

    for h in range(halves):
        for step in range(line - 1):
            for way in range(2):
                @pl.when(w_sends(step, way))
                def _():
                    w_copy(h, step, way).wait_send()
        for d in range(1, group):
            p_copy(h, d).wait_send()
    for d in range(1, group):
        t_copy(d).wait_send()
        for j in range(1, images):
            f_copy(d, j).wait_send()
    for j in range(1, images):
        s_copy(j).wait_send()
    drain(vis_send.at[pl.ds(0, shards - 1)], v_send.at[0])
    drain(pair_send.at[pl.ds(0, shards - 1)], v_send.at[1])
    drain(kv_all.at[pl.ds(0, shards - 1)], v_send.at[2])


def on_device(
    text_states, text_gain, vision, q_weight, k_weight, v_weight, q_gain, k_gain, owners, counts, gate_value,
):
    images = lax.axis_size("img")
    shards = lax.axis_size("fsdp")
    group, halves = 4, 2
    line = shards // group
    rows, width = text_states.shape
    depth, columns = q_weight.shape
    half = columns // halves
    tokens = vision.shape[1]
    head = q_gain.shape[0]
    bf16, f32 = jnp.bfloat16, jnp.float32
    vmem = pl.BlockSpec(memory_space=pltpu.VMEM)
    smem = pl.BlockSpec(memory_space=pltpu.SMEM)
    dma = pltpu.SemaphoreType.DMA
    return pl.pallas_call(
        functools.partial(kernel, images, shards, group, halves),
        out_shape=jax.ShapeDtypeStruct((rows, columns), bf16),
        in_specs=[vmem] * 8 + [smem, smem, vmem],
        out_specs=vmem,
        scratch_shapes=[
            pltpu.VMEM((group, rows, line * depth), bf16),
            pltpu.VMEM((group - 1, rows, line * depth), bf16),
            pltpu.VMEM((halves, line, depth, half), bf16),
            pltpu.VMEM((halves, rows, half), f32),
            pltpu.VMEM((halves, group - 1, rows, half), f32),
            pltpu.VMEM((halves, group - 1, rows, half), f32),
            pltpu.VMEM((shards, tokens, depth), f32),
            pltpu.VMEM((images, shards, tokens, depth), f32),
            pltpu.VMEM((shards, images, tokens, 2 * head), f32),
            pltpu.VMEM((shards, images, tokens, 2 * head), f32),
            pltpu.VMEM((images * tokens, 2 * head), bf16),
            pltpu.VMEM((shards, images * tokens, 2 * head), bf16),
            dma((halves, line - 1, 2)),
            dma((halves, line - 1, 2)),
            dma((group - 1,)),
            dma((group - 1,)),
            dma((group - 1, images - 1)),
            dma((group - 1, images - 1)),
            dma((halves, group - 1)),
            dma((halves, group - 1)),
            dma((3,)),
            dma((3,)),
            dma((images - 1,)),
            dma((images - 1,)),
        ],
        compiler_params=pltpu.CompilerParams(
            collective_id=0, has_side_effects=True, vmem_limit_bytes=56 * 2**20
        ),
    )(
        text_states, text_gain[None], vision, q_weight, k_weight, v_weight, q_gain[None], k_gain[None],
        owners, counts, gate_value[None],
    )


def solution(mesh):
    in_specs = (
        P("fsdp", None),
        P(),
        P("img", "fsdp", None),
        P("fsdp", "img"),
        P("fsdp", "img"),
        P("fsdp", "img"),
        P(),
        P(),
        P("fsdp", None),
        P("fsdp"),
        P(),
    )
    out_specs = P("fsdp", "img")
    return jax.shard_map(
        on_device, mesh=mesh, in_specs=in_specs, out_specs=out_specs, check_vma=False
    )
```

time: 268 us -> 77.7 us (0.29)
  waiting for transfers between devices: 156 us -> 0 us
  blocking collectives: 78.3 us -> 0 us
  Pallas kernels: 0 us -> 73.9 us
  between operations: 14 us -> 0.66 us
  matrix products: 10.8 us -> 0 us
  other arithmetic: 5.62 us -> 0 us
    all_gather x3 -> x0, waiting for transfers between devices: 154 us -> none  [the longest x1 62.2 us: on_device(): lax.all_gather(v_weight, 'fsdp', axis=0, tiled=True)]
    all_gather x3 -> x0, blocking collectives: 78.3 us -> none  [the longest x1 39.4 us: on_device(): key_piece = lax.all_gather(keys, 'fsdp', axis=1, tiled=True)]
    pallas_call x0 -> x1, Pallas kernels: none -> 73.9 us  [on_device(): pl.pallas_call(functools.partial(kernel, images, shards, group, halves),...]
    dot_general x4 -> x0, matrix products: 10.8 us -> none  [the longest x1 7.04 us: on_device(): jnp.dot(columns, lax.all_gather(q_weight, 'fsdp', axis=0, tiled=True), pr...]
    reduce_sum x4 -> x0, other arithmetic: 3.73 us -> none  [the longest x1 3.1 us: on_device(): jnp.mean(text_float * text_float, axis=-1, keepdims=True) + norm_epsilon]
  transfers between devices with their start and end apart: 3 -> 0, of which waited for: 3 -> 0; matrix products, arithmetic and copies ran while one was open for 4% -> 0% of each run, Pallas kernels for 0% -> 0%
where the time goes in v1:
time: 77.7 us; the launch traced here: 76.2 us
  Pallas kernels  73.9 us (95%)
  local copies, waits for them, and re-layouts  1.67 us (2%)
    pallas_call x1, Pallas kernels, on_device(): pl.pallas_call(functools.partial(kernel, images, shards, group, halves),...  73.9 us
    unnamed x1, local copies, waits for them, and re-layouts  1.67 us

profile of v1, /device:TPU:0, one launch (start us, length us, event | category | flops | bytes accessed | tf_op | source)
XLA Modules:
  0.0 76.2 jit_solution(10493256382081693575)
XLA Ops:
  0.7 73.9 %shard_map.109 = bf16[256,512]{1,0:T(8,128)(2,1)} custom-call(bf16[256,8192]{1,0:T(8,128)(2,1)} %text_ref.1, f32[1,8192]{1,0:T(1,128)} %bitcast.5, bf16[1,8,8192]{2,1,0:T(8,128)(2,1)} %vision_ref.1, bf16[512,512]{1,0:T(8,128)(2,1)} %q_ref.1, bf16[512,128]{1,0:T(8,128)(2,1)} %k_ref.1, bf16[512,128]{1,0:T(8,128)(2,1)} %v_ref.1, f32[1,128]{1,0:T(1,128)} %bitcast.6, ...), custom_call_target="tpu_custom_call" | custom-call | tf_op jit(solution)/shard_map/pallas_call | solution.py:293
  74.6 1.7 %copy.14 = bf16[256,512]{1,0:T(8,128)(2,1)} copy(bf16[256,512]{1,0:T(8,128)(2,1)} %shard_map.109) | data formatting | bytes 524288

commit v2 on v1

--- a/solution.py
+++ b/solution.py
@@ -19,24 +19,25 @@
 
 
 def kernel(
-    images, shards, group, halves,
-    text_ref, gain_ref, vision_ref, q_ref, k_ref, v_ref, qg_ref, kg_ref, owners_ref, counts_ref, gate_ref,
+    images, shards, group, halves, pieces,
+    text_hbm, gain_ref, vision_ref, q_ref, k_ref, v_ref, qg_ref, kg_ref, owners_ref, counts_ref, gate_ref,
     out_ref,
-    normed, others, wbuf, total, part_send, part_recv,
+    text_ref, normed, others, wbuf, total, part_send, part_recv,
     vis_send, vis_all, pair_send, pair_recv, kv_own, kv_all,
-    w_send, w_recv, t_send, t_recv, f_send, f_recv, p_send, p_recv, v_send, v_recv, s_send, s_recv,
+    w_send, w_recv, t_send, t_recv, f_send, f_recv, p_send, p_recv, v_send, v_recv, s_send, s_recv, load,
 ):
     img = lax.axis_index("img")
     me = lax.axis_index("fsdp")
     line = shards // group
     along = lax.div(me, group)
     member = lax.rem(me, group)
-    rows, width = text_ref.shape
+    rows, width = text_hbm.shape
     depth, columns = q_ref.shape
     half = columns // halves
     head = qg_ref.shape[1]
     tokens = vision_ref.shape[1]
     part_rows = rows // images
+    piece_rows = part_rows // pieces
 
     def copy(src, dst, send, recv, target):
         return pltpu.make_async_remote_copy(
@@ -55,6 +56,12 @@
     lax.fori_loop(1, shards, greet, 0)
     for j in range(1, images):
         pl.semaphore_signal(barrier, inc=1, device_id={"img": lax.rem(img + j, images)}, device_id_type=MESH)
+    def t_load(j):
+        span = pl.ds(pl.multiple_of(lax.rem(img + j, images) * part_rows, part_rows), part_rows)
+        return pltpu.make_async_copy(text_hbm.at[span], text_ref.at[span], load.at[j])
+
+    for j in range(images):
+        t_load(j).start()
     for h in range(halves):
         wbuf[h, along] = q_ref[:, h * half : (h + 1) * half]
     for f in range(shards):
@@ -123,20 +130,31 @@
             )
         return carry
 
-    lax.fori_loop(0, part_rows // row_tile, norm_all, 0)
-    mine = pl.ds(pl.multiple_of(img * part_rows, part_rows), part_rows)
-
-    def t_copy(d):
-        to = lax.rem(member + d, group)
-        return copy(
-            normed.at[to, mine], others.at[d - 1, mine], t_send.at[d - 1], t_recv.at[d - 1],
+    def partner(d):
+        low = lax.rem(lax.rem(member, 2) + d % 2, 2)
+        high = lax.rem(lax.div(member, 2) + d // 2, 2)
+        return high * 2 + low
+
+    def piece(t):
+        return pl.ds(pl.multiple_of(img * part_rows + t * piece_rows, piece_rows), piece_rows)
+
+    def t_copy(d, t):
+        to = partner(d)
+        return copy(
+            normed.at[to, piece(t)], others.at[d - 1, piece(t)], t_send.at[d - 1, t], t_recv.at[d - 1, t],
             {"fsdp": along * group + to},
         )
 
-    for d in range(1, group):
-        t_copy(d).start()
-
-    for j in range(1, images):
+    t_load(0).wait()
+    steps = piece_rows // row_tile
+    for t in range(pieces):
+        lax.fori_loop(t * steps, (t + 1) * steps, norm_all, 0)
+        for d in range(1, group):
+            t_copy(d, t).start()
+
+    for j in range(1, images):
+        t_load(j).wait()
+
         def norm_own(t, carry):
             row = pl.multiple_of(lax.rem(img + j, images) * part_rows + t * row_tile, row_tile)
             scale = scale_of(row)
@@ -173,47 +191,64 @@
     pair_recv[me] = pair_send[me]
     for step in range(1, line - 1):
         w_arrive(0, step)
-        if step == 1:
-            drain(pair_recv.at[pl.ds(0, shards - 1)], v_recv.at[1])
-            pair = jnp.sum(pair_recv[...], axis=0).reshape(images * tokens, 2 * head)
-            kv_own[:, :head] = head_norm(pair[:, :head], kg_ref[...]).astype(jnp.bfloat16)
-            kv_own[:, head:] = pair[:, head:].astype(jnp.bfloat16)
-            spread(lambda to: kv_own, kv_all.at[me], v_send.at[2], v_recv.at[2])
-            kv_all[me] = kv_own[...]
     w_arrive(1, 0)
 
-    def f_copy(d, j):
-        return copy(
-            others.at[d - 1, mine], others.at[d - 1, mine], f_send.at[d - 1, j - 1], f_recv.at[d - 1, j - 1],
-            {"img": lax.rem(img + j, images)},
-        )
-
+    def f_copy(d, t, j):
+        return copy(
+            others.at[d - 1, piece(t)], others.at[d - 1, piece(t)],
+            f_send.at[d - 1, t, j - 1], f_recv.at[d - 1, t, j - 1], {"img": lax.rem(img + j, images)},
+        )
+
+    def t_arrive(d):
+        for t in range(pieces):
+            t_copy(d, t).wait_recv()
+            for j in range(1, images):
+                f_copy(d, t, j).start()
+
+    def f_arrive(d):
+        for t in range(pieces):
+            for j in range(1, images):
+                f_copy(d, t, j).wait_recv()
+
+    def p_copy(h, d):
+        return copy(
+            part_send.at[h, d - 1], part_recv.at[h, d - 1], p_send.at[h, d - 1], p_recv.at[h, d - 1],
+            {"fsdp": along * group + partner(d)},
+        )
+
+    def project(h, d):
+        weight = wbuf[h].reshape(line * depth, half)
+        product = jnp.dot(
+            normed[member] if d == 0 else others[d - 1], weight, preferred_element_type=jnp.float32
+        )
+        if d == 0:
+            total[h] = product
+        else:
+            part_send[h, d - 1] = product.astype(part_send.dtype)
+            p_copy(h, d).start()
+
+    t_arrive(1)
+    t_arrive(2)
+    f_arrive(1)
+    project(0, 1)
+    f_arrive(2)
+    project(0, 2)
+    w_arrive(1, 1)
+    t_arrive(3)
+    f_arrive(3)
+    project(0, 3)
+    drain(pair_recv.at[pl.ds(0, shards - 1)], v_recv.at[1])
+    pair = jnp.sum(pair_recv[...], axis=0).reshape(images * tokens, 2 * head)
+    kv_own[:, :head] = head_norm(pair[:, :head], kg_ref[...]).astype(jnp.bfloat16)
+    kv_own[:, head:] = pair[:, head:].astype(jnp.bfloat16)
+    spread(lambda to: kv_own, kv_all.at[me], v_send.at[2], v_recv.at[2])
+    kv_all[me] = kv_own[...]
+    project(0, 0)
+    for step in range(2, line - 1):
+        w_arrive(1, step)
     for d in range(1, group):
-        t_copy(d).wait_recv()
-        for j in range(1, images):
-            f_copy(d, j).start()
-    for d in range(1, group):
-        for j in range(1, images):
-            f_copy(d, j).wait_recv()
-
-    def p_copy(h, d):
-        to = lax.rem(member + group - d, group)
-        return copy(
-            part_send.at[h, d - 1], part_recv.at[h, d - 1], p_send.at[h, d - 1], p_recv.at[h, d - 1],
-            {"fsdp": along * group + to},
-        )
-
-    def project(h):
-        weight = wbuf[h].reshape(line * depth, half)
-        for d in range(1, group):
-            part_send[h, d - 1] = jnp.dot(others[d - 1], weight, preferred_element_type=jnp.float32)
-            p_copy(h, d).start()
-        total[h] = jnp.dot(normed[member], weight, preferred_element_type=jnp.float32)
-
-    project(0)
-    for step in range(1, line - 1):
-        w_arrive(1, step)
-    project(1)
+        project(1, d)
+    project(1, 0)
 
     drain(kv_all.at[pl.ds(0, shards - 1)], v_recv.at[2])
     key_count = shards * images * tokens
@@ -242,7 +277,7 @@
             p_copy(h, d).wait_recv()
         full = total[h]
         for d in range(1, group):
-            full = full + part_recv[h, d - 1]
+            full = full + part_recv[h, d - 1].astype(jnp.float32)
         for n in range(half // head):
             queries = head_norm(full[:, n * head : (n + 1) * head], qg_ref[...]).astype(jnp.bfloat16)
             scores = lax.dot_general(
@@ -264,9 +299,10 @@
         for d in range(1, group):
             p_copy(h, d).wait_send()
     for d in range(1, group):
-        t_copy(d).wait_send()
-        for j in range(1, images):
-            f_copy(d, j).wait_send()
+        for t in range(pieces):
+            t_copy(d, t).wait_send()
+            for j in range(1, images):
+                f_copy(d, t, j).wait_send()
     for j in range(1, images):
         s_copy(j).wait_send()
     drain(vis_send.at[pl.ds(0, shards - 1)], v_send.at[0])
@@ -279,7 +315,7 @@
 ):
     images = lax.axis_size("img")
     shards = lax.axis_size("fsdp")
-    group, halves = 4, 2
+    group, halves, pieces = 4, 2, 2
     line = shards // group
     rows, width = text_states.shape
     depth, columns = q_weight.shape
@@ -291,11 +327,12 @@
     smem = pl.BlockSpec(memory_space=pltpu.SMEM)
     dma = pltpu.SemaphoreType.DMA
     return pl.pallas_call(
-        functools.partial(kernel, images, shards, group, halves),
+        functools.partial(kernel, images, shards, group, halves, pieces),
         out_shape=jax.ShapeDtypeStruct((rows, columns), bf16),
-        in_specs=[vmem] * 8 + [smem, smem, vmem],
+        in_specs=[pl.BlockSpec(memory_space=pl.ANY)] + [vmem] * 7 + [smem, smem, vmem],
         out_specs=vmem,
         scratch_shapes=[
+            pltpu.VMEM((rows, width), bf16),
             pltpu.VMEM((group, rows, line * depth), bf16),
             pltpu.VMEM((group - 1, rows, line * depth), bf16),
             pltpu.VMEM((halves, line, depth, half), bf16),
@@ -310,16 +347,17 @@
             pltpu.VMEM((shards, images * tokens, 2 * head), bf16),
             dma((halves, line - 1, 2)),
             dma((halves, line - 1, 2)),
-            dma((group - 1,)),
-            dma((group - 1,)),
-            dma((group - 1, images - 1)),
-            dma((group - 1, images - 1)),
+            dma((group - 1, pieces)),
+            dma((group - 1, pieces)),
+            dma((group - 1, pieces, images - 1)),
+            dma((group - 1, pieces, images - 1)),
             dma((halves, group - 1)),
             dma((halves, group - 1)),
             dma((3,)),
             dma((3,)),
             dma((images - 1,)),
             dma((images - 1,)),
+            dma((images,)),
         ],
         compiler_params=pltpu.CompilerParams(
             collective_id=0, has_side_effects=True, vmem_limit_bytes=56 * 2**20

time: 77.7 us -> 77.1 us (level); the launches traced: 76.2 us -> 76.6 us
  no operation moved by 1% of the time
where the time goes in v2:
time: 77.1 us; the launch traced here: 76.6 us
  Pallas kernels  74.3 us (96%)
  local copies, waits for them, and re-layouts  1.67 us (2%)
    pallas_call x1, Pallas kernels, on_device(): pl.pallas_call(functools.partial(kernel, images, shards, group, halves, p...  74.3 us
    unnamed x1, local copies, waits for them, and re-layouts  1.67 us

profile of v2, /device:TPU:0, one launch (start us, length us, event | category | flops | bytes accessed | tf_op | source)
XLA Modules:
  0.0 76.6 jit_solution(17101105085203559704)
XLA Ops:
  0.7 74.3 %shard_map.109 = bf16[256,512]{1,0:T(8,128)(2,1)} custom-call(bf16[256,8192]{1,0:T(8,128)(2,1)} %text_hbm.1, f32[1,8192]{1,0:T(1,128)} %bitcast.5, bf16[1,8,8192]{2,1,0:T(8,128)(2,1)} %vision_ref.1, bf16[512,512]{1,0:T(8,128)(2,1)} %q_ref.1, bf16[512,128]{1,0:T(8,128)(2,1)} %k_ref.1, bf16[512,128]{1,0:T(8,128)(2,1)} %v_ref.1, f32[1,128]{1,0:T(1,128)} %bitcast.6, ...), custom_call_target="tpu_custom_call" | custom-call | tf_op jit(solution)/shard_map/pallas_call | solution.py:329
  75.0 1.7 %copy.14 = bf16[256,512]{1,0:T(8,128)(2,1)} copy(bf16[256,512]{1,0:T(8,128)(2,1)} %shard_map.109) | data formatting | bytes 524288

commit v3 on v2

--- a/solution.py
+++ b/solution.py
@@ -23,7 +23,7 @@
     text_hbm, gain_ref, vision_ref, q_ref, k_ref, v_ref, qg_ref, kg_ref, owners_ref, counts_ref, gate_ref,
     out_ref,
     text_ref, normed, others, wbuf, total, part_send, part_recv,
-    vis_send, vis_all, pair_send, pair_recv, kv_own, kv_all,
+    vis_send, vis_all, pair_send, pair_recv, pair_plane, pair_near, kv_own, kv_all,
     w_send, w_recv, t_send, t_recv, f_send, f_recv, p_send, p_recv, v_send, v_recv, s_send, s_recv, load,
 ):
     img = lax.axis_index("img")
@@ -185,12 +185,31 @@
         x = vis_all[m].reshape(shards * tokens, depth).astype(jnp.bfloat16)
         keys_part = jnp.dot(x, k_ref[...], preferred_element_type=jnp.float32)
         values_part = jnp.dot(x, v_ref[...], preferred_element_type=jnp.float32)
-        pair_send[:, m, :, :head] = keys_part.reshape(shards, tokens, head)
-        pair_send[:, m, :, head:] = values_part.reshape(shards, tokens, head)
-    spread(lambda to: pair_send.at[to], pair_recv.at[me], v_send.at[1], v_recv.at[1])
-    pair_recv[me] = pair_send[me]
+        pair_send[:, :, m, :, :head] = keys_part.reshape(line, group, tokens, head)
+        pair_send[:, :, m, :, head:] = values_part.reshape(line, group, tokens, head)
+
+    def along_line(source, target, number):
+        def one(step, carry):
+            to = lax.rem(along + step, line)
+            copy(source(to), target, v_send.at[number], v_recv.at[number], {"fsdp": to * group + member}).start()
+            return carry
+
+        lax.fori_loop(1, line, one, 0)
+
+    def over_plane(source, target, number):
+        for d in range(1, group):
+            to = partner(d)
+            copy(
+                source(to), target(d), v_send.at[number], v_recv.at[number], {"fsdp": along * group + to}
+            ).start()
+
+    along_line(lambda to: pair_send.at[to], pair_recv.at[along], 1)
+    pair_recv[along] = pair_send[along]
     for step in range(1, line - 1):
         w_arrive(0, step)
+    drain(pair_recv.at[pl.ds(0, line - 1)], v_recv.at[1])
+    pair_plane[...] = jnp.sum(pair_recv[...], axis=0)
+    over_plane(lambda to: pair_plane.at[to], lambda d: pair_near.at[d - 1], 2)
     w_arrive(1, 0)
 
     def f_copy(d, t, j):
@@ -210,11 +229,16 @@
             for j in range(1, images):
                 f_copy(d, t, j).wait_recv()
 
-    def p_copy(h, d):
+    def p_copy(h, c, number):
+        first, second = (1, 2) if c == 0 else (2, 1)
+        source = (first, 3, second)[number] - 1
+        over = second if number == 2 else first
         return copy(
-            part_send.at[h, d - 1], part_recv.at[h, d - 1], p_send.at[h, d - 1], p_recv.at[h, d - 1],
-            {"fsdp": along * group + partner(d)},
-        )
+            part_send.at[h, c, source], part_recv.at[h, c, number], p_send.at[h, c, number],
+            p_recv.at[h, c, number], {"fsdp": along * group + partner(over)},
+        )
+
+    lane = half // 2
 
     def project(h, d):
         weight = wbuf[h].reshape(line * depth, half)
@@ -223,9 +247,21 @@
         )
         if d == 0:
             total[h] = product
+            return
+        for c in range(2):
+            part_send[h, c, d - 1] = product[:, c * lane : (c + 1) * lane]
+        if d == 3:
+            p_copy(h, 0, 1).start()
+            p_copy(h, 1, 1).start()
         else:
-            part_send[h, d - 1] = product.astype(part_send.dtype)
-            p_copy(h, d).start()
+            p_copy(h, d - 1, 0).start()
+
+    def relay(h):
+        for c in range(2):
+            p_copy(h, c, 1).wait_recv()
+            second = 2 if c == 0 else 1
+            part_send[h, c, second - 1] = part_send[h, c, second - 1] + part_recv[h, c, 1]
+            p_copy(h, c, 2).start()
 
     t_arrive(1)
     t_arrive(2)
@@ -234,23 +270,29 @@
     f_arrive(2)
     project(0, 2)
     w_arrive(1, 1)
+    drain(pair_near, v_recv.at[2])
+    pair = pair_plane[member]
+    for d in range(1, group):
+        pair = pair + pair_near[d - 1]
+    pair = pair.reshape(images * tokens, 2 * head)
+    kv_own[:, :head] = head_norm(pair[:, :head], kg_ref[...]).astype(jnp.bfloat16)
+    kv_own[:, head:] = pair[:, head:].astype(jnp.bfloat16)
+    over_plane(lambda to: kv_own, lambda d: kv_all.at[me], 3)
+    kv_all[me] = kv_own[...]
     t_arrive(3)
     f_arrive(3)
     project(0, 3)
-    drain(pair_recv.at[pl.ds(0, shards - 1)], v_recv.at[1])
-    pair = jnp.sum(pair_recv[...], axis=0).reshape(images * tokens, 2 * head)
-    kv_own[:, :head] = head_norm(pair[:, :head], kg_ref[...]).astype(jnp.bfloat16)
-    kv_own[:, head:] = pair[:, head:].astype(jnp.bfloat16)
-    spread(lambda to: kv_own, kv_all.at[me], v_send.at[2], v_recv.at[2])
-    kv_all[me] = kv_own[...]
     project(0, 0)
     for step in range(2, line - 1):
         w_arrive(1, step)
-    for d in range(1, group):
+    drain(kv_all.at[pl.ds(0, group - 1)], v_recv.at[3])
+    plane = pl.ds(along * group, group)
+    along_line(lambda to: kv_all.at[plane], kv_all.at[plane], 4)
+    relay(0)
+    for d in (3, 1, 2, 0):
         project(1, d)
-    project(1, 0)
-
-    drain(kv_all.at[pl.ds(0, shards - 1)], v_recv.at[2])
+
+    drain(kv_all.at[pl.ds(0, shards - group)], v_recv.at[4])
     key_count = shards * images * tokens
     blocks = owners_ref.shape[0]
     key_image = lax.rem(lax.div(lax.broadcasted_iota(jnp.int32, (1, key_count), 1), tokens), images)
@@ -273,11 +315,14 @@
     pairs = kv_all[...].reshape(key_count, 2 * head)
     keys, values = pairs[:, :head], pairs[:, head:]
     for h in range(halves):
-        for d in range(1, group):
-            p_copy(h, d).wait_recv()
-        full = total[h]
-        for d in range(1, group):
-            full = full + part_recv[h, d - 1].astype(jnp.float32)
+        if h > 0:
+            relay(h)
+        sums = []
+        for c in range(2):
+            p_copy(h, c, 0).wait_recv()
+            p_copy(h, c, 2).wait_recv()
+            sums.append(total[h, :, c * lane : (c + 1) * lane] + part_recv[h, c, 0] + part_recv[h, c, 2])
+        full = jnp.concatenate(sums, axis=1)
         for n in range(half // head):
             queries = head_norm(full[:, n * head : (n + 1) * head], qg_ref[...]).astype(jnp.bfloat16)
             scores = lax.dot_general(
@@ -296,8 +341,9 @@
                 @pl.when(w_sends(step, way))
                 def _():
                     w_copy(h, step, way).wait_send()
-        for d in range(1, group):
-            p_copy(h, d).wait_send()
+        for c in range(2):
+            for number in range(3):
+                p_copy(h, c, number).wait_send()
     for d in range(1, group):
         for t in range(pieces):
             t_copy(d, t).wait_send()
@@ -306,8 +352,10 @@
     for j in range(1, images):
         s_copy(j).wait_send()
     drain(vis_send.at[pl.ds(0, shards - 1)], v_send.at[0])
-    drain(pair_send.at[pl.ds(0, shards - 1)], v_send.at[1])
-    drain(kv_all.at[pl.ds(0, shards - 1)], v_send.at[2])
+    drain(pair_send.at[pl.ds(0, line - 1)], v_send.at[1])
+    drain(pair_near, v_send.at[2])
+    drain(kv_all.at[pl.ds(0, group - 1)], v_send.at[3])
+    drain(kv_all.at[pl.ds(0, shards - group)], v_send.at[4])
 
 
 def on_device(
@@ -337,12 +385,14 @@
             pltpu.VMEM((group - 1, rows, line * depth), bf16),
             pltpu.VMEM((halves, line, depth, half), bf16),
             pltpu.VMEM((halves, rows, half), f32),
-            pltpu.VMEM((halves, group - 1, rows, half), f32),
-            pltpu.VMEM((halves, group - 1, rows, half), f32),
+            pltpu.VMEM((halves, 2, group - 1, rows, half // 2), f32),
+            pltpu.VMEM((halves, 2, group - 1, rows, half // 2), f32),
             pltpu.VMEM((shards, tokens, depth), f32),
             pltpu.VMEM((images, shards, tokens, depth), f32),
-            pltpu.VMEM((shards, images, tokens, 2 * head), f32),
-            pltpu.VMEM((shards, images, tokens, 2 * head), f32),
+            pltpu.VMEM((line, group, images, tokens, 2 * head), f32),
+            pltpu.VMEM((line, group, images, tokens, 2 * head), f32),
+            pltpu.VMEM((group, images, tokens, 2 * head), f32),
+            pltpu.VMEM((group - 1, images, tokens, 2 * head), f32),
             pltpu.VMEM((images * tokens, 2 * head), bf16),
             pltpu.VMEM((shards, images * tokens, 2 * head), bf16),
             dma((halves, line - 1, 2)),
@@ -351,10 +401,10 @@
             dma((group - 1, pieces)),
             dma((group - 1, pieces, images - 1)),
             dma((group - 1, pieces, images - 1)),
-            dma((halves, group - 1)),
-            dma((halves, group - 1)),
-            dma((3,)),
-            dma((3,)),
+            dma((halves, 2, 3)),
+            dma((halves, 2, 3)),
+            dma((5,)),
+            dma((5,)),
             dma((images - 1,)),
             dma((images - 1,)),
             dma((images,)),

time: 77.1 us -> 74.9 us (0.971)
  Pallas kernels: 74.3 us -> 72.4 us
    pallas_call x1, Pallas kernels: 74.3 us -> 72.4 us  [on_device(): pl.pallas_call(functools.partial(kernel, images, shards, group, halves, p...]
where the time goes in v3:
time: 74.9 us; the launch traced here: 74.7 us
  Pallas kernels  72.4 us (97%)
  local copies, waits for them, and re-layouts  1.67 us (2%)
    pallas_call x1, Pallas kernels, on_device(): pl.pallas_call(functools.partial(kernel, images, shards, group, halves, p...  72.4 us
    unnamed x1, local copies, waits for them, and re-layouts  1.67 us

profile of v3, /device:TPU:0, one launch (start us, length us, event | category | flops | bytes accessed | tf_op | source)
XLA Modules:
  0.0 74.7 jit_solution(16602273275005185900)
XLA Ops:
  0.7 72.4 %shard_map.109 = bf16[256,512]{1,0:T(8,128)(2,1)} custom-call(bf16[256,8192]{1,0:T(8,128)(2,1)} %text_hbm.1, f32[1,8192]{1,0:T(1,128)} %bitcast.5, bf16[1,8,8192]{2,1,0:T(8,128)(2,1)} %vision_ref.1, bf16[512,512]{1,0:T(8,128)(2,1)} %q_ref.1, bf16[512,128]{1,0:T(8,128)(2,1)} %k_ref.1, bf16[512,128]{1,0:T(8,128)(2,1)} %v_ref.1, f32[1,128]{1,0:T(1,128)} %bitcast.6, ...), custom_call_target="tpu_custom_call" | custom-call | tf_op jit(solution)/shard_map/pallas_call | solution.py:377
  73.0 1.7 %copy.14 = bf16[256,512]{1,0:T(8,128)(2,1)} copy(bf16[256,512]{1,0:T(8,128)(2,1)} %shard_map.109) | data formatting | bytes 524288

commit v4 on v3

--- a/solution.py
+++ b/solution.py
@@ -19,7 +19,7 @@
 
 
 def kernel(
-    images, shards, group, halves, pieces,
+    images, shards, group, parts, pieces,
     text_hbm, gain_ref, vision_ref, q_ref, k_ref, v_ref, qg_ref, kg_ref, owners_ref, counts_ref, gate_ref,
     out_ref,
     text_ref, normed, others, wbuf, total, part_send, part_recv,
@@ -33,7 +33,7 @@
     member = lax.rem(me, group)
     rows, width = text_hbm.shape
     depth, columns = q_ref.shape
-    half = columns // halves
+    half = columns // parts
     head = qg_ref.shape[1]
     tokens = vision_ref.shape[1]
     part_rows = rows // images
@@ -62,7 +62,7 @@
 
     for j in range(images):
         t_load(j).start()
-    for h in range(halves):
+    for h in range(parts):
         wbuf[h, along] = q_ref[:, h * half : (h + 1) * half]
     for f in range(shards):
         vis_send[f] = vision_ref[0, :, f * depth : (f + 1) * depth].astype(jnp.float32)
@@ -99,6 +99,8 @@
                 w_copy(h, step, way).wait_recv()
         if step + 1 < line - 1:
             w_start(h, step + 1)
+        if step == 0 and h + 2 < parts:
+            w_start(h + 2, 0)
 
     def spread(source, target, send, recv):
         def one(step, carry):
@@ -109,6 +111,7 @@
         lax.fori_loop(1, shards, one, 0)
 
     w_start(0, 0)
+    w_start(1, 0)
     spread(lambda to: vis_send.at[to], vis_all.at[img, me], v_send.at[0], v_recv.at[0])
 
     def scale_of(row):
@@ -149,8 +152,11 @@
     steps = piece_rows // row_tile
     for t in range(pieces):
         lax.fori_loop(t * steps, (t + 1) * steps, norm_all, 0)
-        for d in range(1, group):
+        for d in (1, 2):
             t_copy(d, t).start()
+
+    for t in range(pieces):
+        t_copy(3, t).start()
 
     for j in range(1, images):
         t_load(j).wait()
@@ -178,7 +184,6 @@
     for j in range(1, images):
         s_copy(j).start()
     w_arrive(0, 0)
-    w_start(1, 0)
     for j in range(1, images):
         s_copy(j).wait_recv()
     for m in range(images):
@@ -207,10 +212,11 @@
     pair_recv[along] = pair_send[along]
     for step in range(1, line - 1):
         w_arrive(0, step)
+    for step in range(line - 1):
+        w_arrive(1, step)
     drain(pair_recv.at[pl.ds(0, line - 1)], v_recv.at[1])
     pair_plane[...] = jnp.sum(pair_recv[...], axis=0)
     over_plane(lambda to: pair_plane.at[to], lambda d: pair_near.at[d - 1], 2)
-    w_arrive(1, 0)
 
     def f_copy(d, t, j):
         return copy(
@@ -238,7 +244,7 @@
             p_recv.at[h, c, number], {"fsdp": along * group + partner(over)},
         )
 
-    lane = half // 2
+    lane = rows // 2
 
     def project(h, d):
         weight = wbuf[h].reshape(line * depth, half)
@@ -249,7 +255,7 @@
             total[h] = product
             return
         for c in range(2):
-            part_send[h, c, d - 1] = product[:, c * lane : (c + 1) * lane]
+            part_send[h, c, d - 1] = product[c * lane : (c + 1) * lane]
         if d == 3:
             p_copy(h, 0, 1).start()
             p_copy(h, 1, 1).start()
@@ -265,11 +271,21 @@
 
     t_arrive(1)
     t_arrive(2)
+    w_arrive(2, 0)
     f_arrive(1)
     project(0, 1)
     f_arrive(2)
     project(0, 2)
-    w_arrive(1, 1)
+    w_arrive(2, 1)
+    t_arrive(3)
+    f_arrive(3)
+    project(0, 3)
+    for step in range(2, line - 1):
+        w_arrive(2, step)
+    project(0, 0)
+    for d in (3, 1, 2):
+        project(1, d)
+    w_arrive(3, 0)
     drain(pair_near, v_recv.at[2])
     pair = pair_plane[member]
     for d in range(1, group):
@@ -279,18 +295,20 @@
     kv_own[:, head:] = pair[:, head:].astype(jnp.bfloat16)
     over_plane(lambda to: kv_own, lambda d: kv_all.at[me], 3)
     kv_all[me] = kv_own[...]
-    t_arrive(3)
-    f_arrive(3)
-    project(0, 3)
-    project(0, 0)
-    for step in range(2, line - 1):
-        w_arrive(1, step)
+    project(1, 0)
+    relay(0)
+    w_arrive(3, 1)
+    for d in (3, 1, 2, 0):
+        project(2, d)
+    relay(1)
     drain(kv_all.at[pl.ds(0, group - 1)], v_recv.at[3])
     plane = pl.ds(along * group, group)
     along_line(lambda to: kv_all.at[plane], kv_all.at[plane], 4)
-    relay(0)
+    for step in range(2, line - 1):
+        w_arrive(3, step)
     for d in (3, 1, 2, 0):
-        project(1, d)
+        project(3, d)
+    relay(2)
 
     drain(kv_all.at[pl.ds(0, shards - group)], v_recv.at[4])
     key_count = shards * images * tokens
@@ -314,15 +332,15 @@
     factor = jnp.concatenate(factors, axis=0)
     pairs = kv_all[...].reshape(key_count, 2 * head)
     keys, values = pairs[:, :head], pairs[:, head:]
-    for h in range(halves):
-        if h > 0:
-            relay(h)
+    for h in range(parts):
+        if h == parts - 2:
+            relay(h + 1)
         sums = []
         for c in range(2):
             p_copy(h, c, 0).wait_recv()
             p_copy(h, c, 2).wait_recv()
-            sums.append(total[h, :, c * lane : (c + 1) * lane] + part_recv[h, c, 0] + part_recv[h, c, 2])
-        full = jnp.concatenate(sums, axis=1)
+            sums.append(total[h, c * lane : (c + 1) * lane] + part_recv[h, c, 0] + part_recv[h, c, 2])
+        full = jnp.concatenate(sums, axis=0)
         for n in range(half // head):
             queries = head_norm(full[:, n * head : (n + 1) * head], qg_ref[...]).astype(jnp.bfloat16)
             scores = lax.dot_general(
@@ -335,7 +353,7 @@
             place = h * half + n * head
             out_ref[:, place : place + head] = (numerator / denominator * factor).astype(jnp.bfloat16)
 
-    for h in range(halves):
+    for h in range(parts):
         for step in range(line - 1):
             for way in range(2):
                 @pl.when(w_sends(step, way))
@@ -363,11 +381,11 @@
 ):
     images = lax.axis_size("img")
     shards = lax.axis_size("fsdp")
-    group, halves, pieces = 4, 2, 2
+    group, parts, pieces = 4, 4, 2
     line = shards // group
     rows, width = text_states.shape
     depth, columns = q_weight.shape
-    half = columns // halves
+    half = columns // parts
     tokens = vision.shape[1]
     head = q_gain.shape[0]
     bf16, f32 = jnp.bfloat16, jnp.float32
@@ -375,7 +393,7 @@
     smem = pl.BlockSpec(memory_space=pltpu.SMEM)
     dma = pltpu.SemaphoreType.DMA
     return pl.pallas_call(
-        functools.partial(kernel, images, shards, group, halves, pieces),
+        functools.partial(kernel, images, shards, group, parts, pieces),
         out_shape=jax.ShapeDtypeStruct((rows, columns), bf16),
         in_specs=[pl.BlockSpec(memory_space=pl.ANY)] + [vmem] * 7 + [smem, smem, vmem],
         out_specs=vmem,
@@ -383,10 +401,10 @@
             pltpu.VMEM((rows, width), bf16),
             pltpu.VMEM((group, rows, line * depth), bf16),
             pltpu.VMEM((group - 1, rows, line * depth), bf16),
-            pltpu.VMEM((halves, line, depth, half), bf16),
-            pltpu.VMEM((halves, rows, half), f32),
-            pltpu.VMEM((halves, 2, group - 1, rows, half // 2), f32),
-            pltpu.VMEM((halves, 2, group - 1, rows, half // 2), f32),
+            pltpu.VMEM((parts, line, depth, half), bf16),
+            pltpu.VMEM((parts, rows, half), f32),
+            pltpu.VMEM((parts, 2, group - 1, rows // 2, half), f32),
+            pltpu.VMEM((parts, 2, group - 1, rows // 2, half), f32),
             pltpu.VMEM((shards, tokens, depth), f32),
             pltpu.VMEM((images, shards, tokens, depth), f32),
             pltpu.VMEM((line, group, images, tokens, 2 * head), f32),
@@ -395,14 +413,14 @@
             pltpu.VMEM((group - 1, images, tokens, 2 * head), f32),
             pltpu.VMEM((images * tokens, 2 * head), bf16),
             pltpu.VMEM((shards, images * tokens, 2 * head), bf16),
-            dma((halves, line - 1, 2)),
-            dma((halves, line - 1, 2)),
+            dma((parts, line - 1, 2)),
+            dma((parts, line - 1, 2)),
             dma((group - 1, pieces)),
             dma((group - 1, pieces)),
             dma((group - 1, pieces, images - 1)),
             dma((group - 1, pieces, images - 1)),
-            dma((halves, 2, 3)),
-            dma((halves, 2, 3)),
+            dma((parts, 2, 3)),
+            dma((parts, 2, 3)),
             dma((5,)),
             dma((5,)),
             dma((images - 1,)),

time: 74.9 us -> 72.3 us (0.965)
  Pallas kernels: 72.4 us -> 69.8 us
    pallas_call x1, Pallas kernels: 72.4 us -> 69.8 us  [on_device(): pl.pallas_call(functools.partial(kernel, images, shards, group, parts, pi...]
where the time goes in v4:
time: 72.3 us; the launch traced here: 72.1 us
  Pallas kernels  69.8 us (97%)
  local copies, waits for them, and re-layouts  1.67 us (2%)
    pallas_call x1, Pallas kernels, on_device(): pl.pallas_call(functools.partial(kernel, images, shards, group, parts, pi...  69.8 us
    unnamed x1, local copies, waits for them, and re-layouts  1.67 us

profile of v4, /device:TPU:0, one launch (start us, length us, event | category | flops | bytes accessed | tf_op | source)
XLA Modules:
  0.0 72.1 jit_solution(9635088138193570986)
XLA Ops:
  0.7 69.8 %shard_map.109 = bf16[256,512]{1,0:T(8,128)(2,1)} custom-call(bf16[256,8192]{1,0:T(8,128)(2,1)} %text_hbm.1, f32[1,8192]{1,0:T(1,128)} %bitcast.5, bf16[1,8,8192]{2,1,0:T(8,128)(2,1)} %vision_ref.1, bf16[512,512]{1,0:T(8,128)(2,1)} %q_ref.1, bf16[512,128]{1,0:T(8,128)(2,1)} %k_ref.1, bf16[512,128]{1,0:T(8,128)(2,1)} %v_ref.1, f32[1,128]{1,0:T(1,128)} %bitcast.6, ...), custom_call_target="tpu_custom_call" | custom-call | tf_op jit(solution)/shard_map/pallas_call | solution.py:395
  70.4 1.7 %copy.14 = bf16[256,512]{1,0:T(8,128)(2,1)} copy(bf16[256,512]{1,0:T(8,128)(2,1)} %shard_map.109) | data formatting | bytes 524288

commit v5 on v4

--- a/solution.py
+++ b/solution.py
@@ -24,7 +24,7 @@
     out_ref,
     text_ref, normed, others, wbuf, total, part_send, part_recv,
     vis_send, vis_all, pair_send, pair_recv, pair_plane, pair_near, kv_own, kv_all,
-    w_send, w_recv, t_send, t_recv, f_send, f_recv, p_send, p_recv, v_send, v_recv, s_send, s_recv, load,
+    w_send, w_recv, t_send, t_recv, f_send, f_recv, p_send, p_recv, v_send, v_recv, s_send, s_recv, load, hop, h_send, h_recv,
 ):
     img = lax.axis_index("img")
     me = lax.axis_index("fsdp")
@@ -142,10 +142,17 @@
         return pl.ds(pl.multiple_of(img * part_rows + t * piece_rows, piece_rows), piece_rows)
 
     def t_copy(d, t):
-        to = partner(d)
-        return copy(
-            normed.at[to, piece(t)], others.at[d - 1, piece(t)], t_send.at[d - 1, t], t_recv.at[d - 1, t],
+        to = partner(d if d < 3 else 2 - t)
+        source = normed.at[to, piece(t)] if d < 3 else hop.at[t]
+        return copy(
+            source, others.at[d - 1, piece(t)], t_send.at[d - 1, t], t_recv.at[d - 1, t],
             {"fsdp": along * group + to},
+        )
+
+    def h_copy(t):
+        return copy(
+            normed.at[partner(3), piece(t)], hop.at[t], h_send.at[t], h_recv.at[t],
+            {"fsdp": along * group + partner(t + 1)},
         )
 
     t_load(0).wait()
@@ -156,7 +163,7 @@
             t_copy(d, t).start()
 
     for t in range(pieces):
-        t_copy(3, t).start()
+        h_copy(t).start()
 
     for j in range(1, images):
         t_load(j).wait()
@@ -271,6 +278,9 @@
 
     t_arrive(1)
     t_arrive(2)
+    for t in range(pieces):
+        h_copy(t).wait_recv()
+        t_copy(3, t).start()
     w_arrive(2, 0)
     f_arrive(1)
     project(0, 1)
@@ -367,6 +377,8 @@
             t_copy(d, t).wait_send()
             for j in range(1, images):
                 f_copy(d, t, j).wait_send()
+    for t in range(pieces):
+        h_copy(t).wait_send()
     for j in range(1, images):
         s_copy(j).wait_send()
     drain(vis_send.at[pl.ds(0, shards - 1)], v_send.at[0])
@@ -426,6 +438,9 @@
             dma((images - 1,)),
             dma((images - 1,)),
             dma((images,)),
+            pltpu.VMEM((pieces, rows // images // pieces, line * depth), bf16),
+            dma((pieces,)),
+            dma((pieces,)),
         ],
         compiler_params=pltpu.CompilerParams(
             collective_id=0, has_side_effects=True, vmem_limit_bytes=56 * 2**20

time: 72.3 us -> 74.5 us (1.030)
  Pallas kernels: 69.8 us -> 71.8 us
    pallas_call x1, Pallas kernels: 69.8 us -> 71.8 us  [on_device(): pl.pallas_call(functools.partial(kernel, images, shards, group, parts, pi...]
where the time goes in v5:
time: 74.5 us; the launch traced here: 74.1 us
  Pallas kernels  71.8 us (96%)
  local copies, waits for them, and re-layouts  1.67 us (2%)
    pallas_call x1, Pallas kernels, on_device(): pl.pallas_call(functools.partial(kernel, images, shards, group, parts, pi...  71.8 us
    unnamed x1, local copies, waits for them, and re-layouts  1.67 us

profile of v5, /device:TPU:0, one launch (start us, length us, event | category | flops | bytes accessed | tf_op | source)
XLA Modules:
  0.0 74.1 jit_solution(1385732146025539116)
XLA Ops:
  0.7 71.8 %shard_map.109 = bf16[256,512]{1,0:T(8,128)(2,1)} custom-call(bf16[256,8192]{1,0:T(8,128)(2,1)} %text_hbm.1, f32[1,8192]{1,0:T(1,128)} %bitcast.5, bf16[1,8,8192]{2,1,0:T(8,128)(2,1)} %vision_ref.1, bf16[512,512]{1,0:T(8,128)(2,1)} %q_ref.1, bf16[512,128]{1,0:T(8,128)(2,1)} %k_ref.1, bf16[512,128]{1,0:T(8,128)(2,1)} %v_ref.1, f32[1,128]{1,0:T(1,128)} %bitcast.6, ...), custom_call_target="tpu_custom_call" | custom-call | tf_op jit(solution)/shard_map/pallas_call | solution.py:407
  72.5 1.7 %copy.14 = bf16[256,512]{1,0:T(8,128)(2,1)} copy(bf16[256,512]{1,0:T(8,128)(2,1)} %shard_map.109) | data formatting | bytes 524288
